TPU v7x, 32 devices: a whole 2x2x4 slice. The times are simulated.
32 devices in a mesh: groups: 2 (over y), img: 4 (over z), dsc: 2 (over x), rep: 2 (over core).
Axes of the slice: x: 2, y: 2, z: 4, core: 2. Of those that a mesh axis runs over, the one named last changes fastest.
Arguments:
- images: bfloat16 [2048, 2048], P(('groups', 'img'), 'dsc'), parts along dimension 0, may hold values from -6 to 6
- neighbours: int32 [2048, 10], P(('groups', 'img')), parts along dimension 0, may hold values from 0 to 1023, as said below
- similarity: float32 [2048, 10], P(('groups', 'img')), parts along dimension 0, may hold values from 0.3 to 1
- queries: bfloat16 [16384, 2048], P(('groups', 'rep'), 'dsc'), parts along dimension 0, may hold values from -6 to 6
- shortlist: int32 [16384, 2], P(('groups', 'rep')), parts along dimension 0, may hold values from 0 to 7, as said below
Outputs:
- augmented: bfloat16 [2048, 2048], P(('groups', 'img'), 'dsc'), parts along dimension 0
- scores: float32 [2, 8192, 256], P('rep', ('groups', 'img', 'dsc')), parts along dimension 1
There are 2 independent parts, one for each index of `groups`. A program takes and returns all parts, laid end to end along the dimension named above; each array names one. Nothing has to cross between parts.
Inputs may be any that keep to these rules, and one draw needn't show every extreme that they name: `neighbours`: among the neighbour entries of the 128 rows of one aligned half of an image block, at most 640 name images of one image block of 256 ids (ids i * 256 to (i + 1) * 256 - 1); in every half some image block is named exactly 640 times, and both halves of an image block name the same image block that often. Split the queries into aligned groups of 512 (queries g * 512 to (g + 1) * 512 - 1). Among the 1024 shortlist entries of one group, at most 512 name blocks whose images lie in one image block of 256 ids; in every group some image block is named exactly 512 times.
All inputs are finite; a program needn't handle non-finite values.
Results may differ from a plain program's by a relative error of at most 0.0029.
Values may be sent and summed in bfloat16 or wider, within the bound.
A program may use at most 128 MiB of HBM per device.

v0:
```python
import jax
import jax.numpy as jnp
from jax import lax
from jax.sharding import PartitionSpec as P

BLK = 128


epsilon = 1e-06


def fetch_rows(neighbour_ids, images, capacity):
    owners_count = lax.axis_size("img")
    rows_dev = images.shape[0]
    flat_ids = neighbour_ids.reshape(-1)
    owner = flat_ids // rows_dev
    local_row = flat_ids % rows_dev
    member = (owner[:, None] == jnp.arange(owners_count, dtype=jnp.int32)[None, :]).astype(
        jnp.int32
    )
    earlier = jnp.cumsum(member, axis=0) - member
    slot = jnp.sum(earlier * member, axis=1)
    request = jnp.zeros((owners_count, capacity), jnp.int32).at[owner, slot].set(local_row)
    picked = jnp.take(
        images, lax.all_to_all(request, "img", split_axis=0, concat_axis=0, tiled=True), axis=0
    )
    fetched = lax.all_to_all(picked, "img", split_axis=0, concat_axis=0, tiled=True)
    gathered = fetched[owner, slot]
    return gathered.reshape(neighbour_ids.shape[0], neighbour_ids.shape[1], images.shape[1])


def blend_rows(own_rows, picked, weights):
    total = own_rows.astype(jnp.float32)
    for column in range(weights.shape[1]):
        total = total + weights[:, column : column + 1] * picked[:, column].astype(jnp.float32)
    return total


def per_device(images, neighbours, similarity, queries, shortlist):
    owners_count = lax.axis_size("img")
    rows_dev = images.shape[0]
    half_rows = rows_dev // 2
    half_capacity = 2 * half_rows * neighbours.shape[1] // owners_count
    capacity = 2 * half_capacity
    weights = similarity**3
    picked = fetch_rows(neighbours, images, capacity)
    summed = blend_rows(images, picked, weights)
    squares = lax.psum(jnp.sum(summed * summed, axis=1), "dsc")
    normed = (summed * lax.rsqrt(squares + epsilon)[:, None]).astype(jnp.bfloat16)
    blocks_dev = rows_dev // BLK
    first_block = lax.axis_index("img") * blocks_dev
    own_count = queries.shape[0] // (lax.axis_size("img") * lax.axis_size("dsc"))
    step_rows = 512
    query_blocks = queries.reshape(
        lax.axis_size(("img", "dsc")) * own_count // step_rows, step_rows, queries.shape[1]
    )
    list_blocks = shortlist.reshape(
        lax.axis_size(("img", "dsc")) * own_count // step_rows, step_rows, shortlist.shape[1]
    )

    def score_block(pair):
        query_part, list_part = pair
        select = (
            (list_part - first_block)[:, :, None]
            == jnp.arange(blocks_dev, dtype=jnp.int32)[None, None, :]
        ).astype(jnp.float32)
        dense = jnp.einsum("qd,nd->qn", query_part, normed, preferred_element_type=jnp.float32)
        dense = dense.reshape(step_rows, blocks_dev, BLK)
        chosen = jnp.einsum("qsp,qpb->qsb", select, dense, precision=lax.Precision.HIGHEST)
        return chosen.reshape(step_rows, -1)

    scores = lax.psum_scatter(
        lax.map(score_block, (query_blocks, list_blocks)).reshape(
            lax.axis_size(("img", "dsc")) * own_count, -1
        ),
        ("img", "dsc"),
        scatter_dimension=0,
        tiled=True,
    )
    return (normed, scores[None])


def solution(mesh):
    placed = (
        P(("groups", "img"), "dsc"),
        P(("groups", "img"), None),
        P(("groups", "img"), None),
        P(("groups", "rep"), "dsc"),
        P(("groups", "rep"), None),
    )
    return jax.shard_map(
        per_device,
        mesh=mesh,
        in_specs=placed,
        out_specs=(P(("groups", "img"), "dsc"), P("rep", ("groups", "img", "dsc"), None)),
        check_vma=False,
    )
```

profile of v0, /device:TPU:0, one launch (start us, length us, event | category | flops | bytes accessed | tf_op | source)
XLA Modules:
  0.0 551.4 jit_solution(4913256899622929745)
XLA Ops:
  8.5 1.2 reduce-window.6
  11.9 9.9 %scatter_custom_fusion = s32[5120]{0:T(1024)S(1)} fusion(s32[2560]{0:T(1024)S(1)} %broadcast_select_fusion.1, s32[2560]{0:T(1024)S(1)} %get-tuple-element.72, s32[]{:T(128)} %copy.111), kind=kCustom, calls=%fused_computation.85 | custom fusion | bytes 20484
  21.9 11.7 %all_to_all.20 = s32[4,1,1280]{2,1,0:T(1,128)S(1)} all-to-all(s32[4,1,1280]{2,1,0:T(1,128)S(1)} %bitcast.121), channel_id=1, replica_groups=mesh['groups'=2,'img'=4,'dsc'=2,'rep'=2] {'img'}, dimensions={0} | all-to-all | bytes 40960 | tf_op jit(solution)/shard_map/all_to_all | solution.py:25
  33.7 22.6 %gather_fusion = bf16[5120,1024]{1,0:T(8,128)(2,1)} fusion(bf16[256,1024]{1,0:T(8,128)(2,1)S(1)} %copy-done, s32[5120]{0:T(1024)S(1)} %broadcast_clamp_fusion), kind=kCustom, calls=%fused_computation | custom fusion | bytes 20992000 | tf_op jit(solution)/shard_map/jit(_take)/gather | solution.py:24
  56.3 10.1 %broadcast_select_fusion = bf16[4,1280,1024]{2,1,0:T(8,128)(2,1)} fusion(bf16[4,1280,1024]{2,1,0:T(8,128)(2,1)} %bitcast.117, pred[4,1280]{1,0:T(4,128)(4,1)S(1)} %compare_and_fusion), kind=kLoop, calls=%fused_computation.14 | loop fusion | flops 5242880 | bytes 20976640 | tf_op jit(solution)/shard_map/jit(_take)/select_n | solution.py:24
  66.4 6.1 %all-to-all-start.1 = ((bf16[4,1280,1024]{2,1,0:T(8,128)(2,1)}), bf16[4,1280,1024]{2,1,0:T(8,128)(2,1)}, u32[]{:S(2)}, u32[]{:S(2)}) async-start(bf16[4,1280,1024]{2,1,0:T(8,128)(2,1)} %broadcast_select_fusion), calls=%async_computation.1 | async-start | bytes 20971520 | tf_op jit(solution)/shard_map/all_to_all | solution.py:27
  72.6 2.1 copy.44
  74.7 224.7 %all-to-all-done.1 = bf16[4,1280,1024]{2,1,0:T(8,128)(2,1)} async-done(((bf16[4,1280,1024]{2,1,0:T(8,128)(2,1)}), bf16[4,1280,1024]{2,1,0:T(8,128)(2,1)}, u32[]{:S(2)}, u32[]{:S(2)}) %all-to-all-start.1) | async-done | bytes 10485792 | tf_op jit(solution)/shard_map/all_to_all | solution.py:27
  299.4 51.6 %gather_fusion.1 = bf16[2560,1024]{1,0:T(8,128)(2,1)} fusion(bf16[4,1280,1024]{2,1,0:T(8,128)(2,1)} %all-to-all-done.1, s32[2560]{0:T(1024)S(1)} %get-tuple-element.49), kind=kCustom, calls=%fused_computation.1 | custom fusion | bytes 10506240 | tf_op jit(solution)/shard_map/gather | solution.py:28
  351.0 10.5 %reshape.216 = bf16[256,10,1024]{2,1,0:T(8,128)(2,1)} reshape(bf16[2560,1024]{1,0:T(8,128)(2,1)} %gather_fusion.1) | data formatting | bytes 10485760 | tf_op jit(solution)/shard_map/reshape | solution.py:29
  361.5 20.8 %fusion.30 = (bf16[256,1,1024]{2,1,0:T(2,128)(2,1)S(1)}, bf16[256,1,1024]{2,1,0:T(2,128)(2,1)S(1)}, bf16[256,1,1024]{2,1,0:T(2,128)(2,1)S(1)}, bf16[256,1,1024]{...) fusion(bf16[256,10,1024]{2,1,0:T(8,128)(2,1)} %reshape.216), kind=kLoop, calls=%fused_computation.90 | loop fusion | flops 262144 | bytes 11010048 | tf_op jit(solution)/shard_map/slice | solution.py:35
  382.3 2.2 multiply_reduce_fusion
  384.5 4.9 psum.7
  389.6 67.7 %while.10 = (s32[]{:T(128)}, f32[8,512,256]{2,1,0:T(8,128)}, s32[8,512,2]{2,1,0:T(8,128)}, s32[]{:T(128)}, bf16[8,512,1024]{2,1,0:T(8,128)(2,1)}, /*index=5*/bf16[256,1024]{1,0:T(8,128)(2,1)S(1)}, s32[]{:T(128)}) while((s32[]{:T(128)}, f32[8,512,256]{2,1,0:T(8,128)}, s32[8,512,2]{2,1,0:T(8,128)}, s32[]{:T(128)}, ...), condition=%wide.region_7.8_spmd, body=%wide.region_6.7_spmd.sunk | while | flops 271584256 | bytes 5256277 | solution.py:73
  389.6 1.7 fusion.43
  391.3 1.0 subtract_bitcast_fusion.2
  392.3 4.5 fusion.44
  398.0 1.7 fusion.43
  400.7 4.5 fusion.44
  406.5 1.7 fusion.43
  409.2 4.5 fusion.44
  415.0 1.7 fusion.43
  417.7 4.5 fusion.44
  423.5 1.7 fusion.43
  426.1 4.5 fusion.44
  431.9 1.7 fusion.43
  434.6 4.5 fusion.44
  440.4 1.7 fusion.43
  443.1 4.5 fusion.44
  448.9 1.7 fusion.43
  451.5 4.5 fusion.44
  457.3 87.2 %reduce-scatter.2.cloned.1.call-done = f32[512,256]{1,0:T(8,128)} async-done(((f32[4096,256]{1,0:T(8,128)}), f32[512,256]{1,0:T(8,128)}) %reduce-scatter.2.cloned.1.call-update) | async-done | bytes 524304 | tf_op jit(solution)/shard_map/reduce_scatter | solution.py:72
  (56 shorter events, 20.8 us)
Async XLA Ops:
  7.2 26.5 %copy-start = (bf16[256,1024]{1,0:T(8,128)(2,1)S(1)}, bf16[256,1024]{1,0:T(8,128)(2,1)}, u32[]{:S(2)}) copy-start(bf16[256,1024]{1,0:T(8,128)(2,1)} %param.7) | copy-start | bytes 1572868
  66.4 6.2 %copy-start.2 = (s32[4096,2]{0,1:T(2,128)S(1)}, s32[4096,2]{0,1:T(2,128)}, u32[]{:S(2)}) copy-start(s32[4096,2]{0,1:T(2,128)} %param.11) | copy-start | bytes 98308
  66.4 8.3 %copy-start.3 = (f32[256,10]{0,1:T(8,128)S(1)}, f32[256,10]{0,1:T(8,128)}, u32[]{:S(2)}) copy-start(f32[256,10]{0,1:T(8,128)} %param.9) | copy-start | bytes 30724
  66.4 233.0 %all-to-all-start.1 = ((bf16[4,1280,1024]{2,1,0:T(8,128)(2,1)}), bf16[4,1280,1024]{2,1,0:T(8,128)(2,1)}, u32[]{:S(2)}, u32[]{:S(2)}) async-start(bf16[4,1280,1024]{2,1,0:T(8,128)(2,1)} %broadcast_select_fusion), calls=%async_computation.1 | async-start | bytes 20971520 | tf_op jit(solution)/shard_map/all_to_all | solution.py:27
  72.5 472.1 %reduce-scatter.2.cloned.1.call-start = ((), (), s32[]{:S(2)}) async-start(), calls=%async_computation.3 | async-start | bytes 4718592 | tf_op jit(solution)/shard_map/reduce_scatter | solution.py:72
  457.3 87.3 %copy-start.1 = (bf16[256,1024]{1,0:T(8,128)(2,1)}, bf16[256,1024]{1,0:T(8,128)(2,1)S(1)}, u32[]{:S(2)}) copy-start(bf16[256,1024]{1,0:T(8,128)(2,1)S(1)} %get-tuple-element.135) | copy-start | bytes 1572868
Sparse Core Ops, SparseCore 0:
  457.5 87.0 reduce-scatter.1
where the time goes:
time: 553 us; the launch traced here: 551 us
  waiting for transfers between devices  312 us (56%)
  local copies, waits for them, and re-layouts  108 us (20%)
  matrix products  49.6 us (9%)
  other arithmetic  44.3 us (8%)
  blocking collectives  16.7 us (3%)
  between operations  14.2 us (3%)
  starting transfers between devices  6.16 us (1%)
    all_to_all x1, waiting for transfers between devices, fetch_rows(): lax.all_to_all(picked, 'img', split_axis=0, concat_axis=0, tiled=True)  225 us
    reduce_scatter x1, waiting for transfers between devices, per_device(): lax.psum_scatter(lax.map(score_block, (query_blocks, list_blocks)).reshap...  87.2 us
    gather x1, local copies, waits for them, and re-layouts, fetch_rows(): gathered = fetched[owner, slot]  51.6 us
    dot_general x8, matrix products, score_block(): jnp.einsum('qsp,qpb->qsb', select, dense, precision=lax.Precision.HIGHEST)  36 us
    gather x1, local copies, waits for them, and re-layouts, fetch_rows(): jnp.take(images, lax.all_to_all(request, 'img', split_axis=0, concat_axis...  22.6 us
    slice x1, other arithmetic, blend_rows(): picked[:, column].astype(jnp.float32)  20.8 us
    dot_general x8, matrix products, score_block(): jnp.einsum('qd,nd->qn', query_part, normed, preferred_element_type=jnp.fl...  13.6 us
    unnamed x11, local copies, waits for them, and re-layouts  12.9 us
  transfers between devices with their start and end apart: 2, of which 2 were waited for; matrix products, arithmetic and copies ran while one was open for 0% of the time, Pallas kernels for 0%

commit v1 on v0

v1 whole, which is shorter than its diff:
```python
import functools

import jax
import jax.numpy as jnp
from jax import lax
from jax.experimental import pallas as pl
from jax.experimental.pallas import tpu as pltpu
from jax.sharding import PartitionSpec as P

BLK = 128
MESH = pl.DeviceIdType.MESH
epsilon = 1e-06


def each(count, body):
    if count <= 4:
        for index in range(count):
            body(index)
    else:

        def step(index, carry):
            body(index)
            return carry

        lax.fori_loop(0, count, step, 0)


def kernel(
    n_img, n_dsc, n_near, n_chunk, n_part, stored,
    img_ref, meta_ref, list_ref, q_hbm,
    aug_out, score_out,
    gath, metas, wt, acc, augt, sqs, qv, send_buf, recv_buf,
    q_sem, meta_send, meta_recv, z_right, z_left, z_recv, sib_send, sib_recv,
    sq_send, sq_recv, part_send, part_recv,
):
    me = lax.axis_index("img")
    my_d = lax.axis_index("dsc")
    my_r = lax.axis_index("rep")
    sib = 1 - my_r
    rows = img_ref.shape[0]
    n_block, width = gath.shape[1], gath.shape[2]
    part_rows = qv.shape[1]

    barrier = pltpu.get_barrier_semaphore()
    for t in range(1, n_img):
        pl.semaphore_signal(
            barrier, inc=1, device_id={"img": lax.rem(me + t, n_img)}, device_id_type=MESH
        )
    for t in range(1, n_dsc):
        pl.semaphore_signal(
            barrier, inc=1, device_id={"dsc": lax.rem(my_d + t, n_dsc)}, device_id_type=MESH
        )
    pl.semaphore_signal(barrier, inc=1, device_id={"rep": sib}, device_id_type=MESH)

    q_copy = pltpu.make_async_copy(q_hbm.at[me], qv, q_sem)
    q_copy.start()
    metas[me] = meta_ref[...]
    for b in range(n_block):
        gath[me, b] = img_ref[:, b * width : (b + 1) * width].T
    pl.semaphore_wait(barrier, n_img + n_dsc - 1)

    def meta_copy(t):
        return pltpu.make_async_remote_copy(
            src_ref=metas.at[me], dst_ref=metas.at[me],
            send_sem=meta_send.at[t], recv_sem=meta_recv.at[me],
            device_id={"img": lax.rem(me + t, n_img)}, device_id_type=MESH,
        )

    def meta_wait(p):
        pltpu.make_async_remote_copy(
            src_ref=metas.at[p], dst_ref=metas.at[p],
            send_sem=meta_send.at[0], recv_sem=meta_recv.at[p],
            device_id={"rep": sib}, device_id_type=MESH,
        ).wait_recv()

    def z_copy(p, c, side):
        piece = gath.at[p, my_r * n_chunk + c]
        return pltpu.make_async_remote_copy(
            src_ref=piece, dst_ref=piece,
            send_sem=(z_right if side > 0 else z_left).at[p, c], recv_sem=z_recv.at[p, c],
            device_id={"img": me + side}, device_id_type=MESH,
        )

    def z_wait(p, c):
        piece = gath.at[p, my_r * n_chunk + c]
        pltpu.make_async_remote_copy(
            src_ref=piece, dst_ref=piece,
            send_sem=z_right.at[p, c], recv_sem=z_recv.at[p, c],
            device_id={"rep": sib}, device_id_type=MESH,
        ).wait_recv()

    def sib_copy(p, c):
        piece = gath.at[p, my_r * n_chunk + c]
        return pltpu.make_async_remote_copy(
            src_ref=piece, dst_ref=piece,
            send_sem=sib_send.at[p, c], recv_sem=sib_recv.at[p, c],
            device_id={"rep": sib}, device_id_type=MESH,
        )

    def sib_wait(p, c):
        piece = gath.at[p, sib * n_chunk + c]
        pltpu.make_async_remote_copy(
            src_ref=piece, dst_ref=piece,
            send_sem=sib_send.at[p, c], recv_sem=sib_recv.at[p, c],
            device_id={"rep": sib}, device_id_type=MESH,
        ).wait_recv()

    for t in range(1, n_img):
        meta_copy(t).start()
    has_right, has_left = me + 1 < n_img, me > 0
    for c in range(n_chunk):

        @pl.when(has_right)
        def _():
            z_copy(me, c, 1).start()

        @pl.when(has_left)
        def _():
            z_copy(me, c, -1).start()

    def event(t, c):
        @pl.when(me >= t)
        def _():
            z_wait(me - t, c)

            @pl.when(has_right)
            def _():
                z_copy(me - t, c, 1).start()

            sib_copy(me - t, c).start()

        @pl.when(me + t < n_img)
        def _():
            z_wait(me + t, c)

            @pl.when(has_left)
            def _():
                z_copy(me + t, c, -1).start()

            sib_copy(me + t, c).start()

    def build(target, source, put):
        sub = 64
        lane = lax.broadcasted_iota(jnp.int32, (sub, rows), 1) + target * rows
        line = lax.broadcasted_iota(jnp.int32, (sub, rows), 0) + source * rows
        for j in range(rows // sub):
            here = line + j * sub
            value = jnp.where(here == lane, 1.0, 0.0)
            ids = here.astype(jnp.float32)
            for k in range(n_near):
                weight = metas[target, k : k + 1, :]
                near = metas[target, n_near + k : n_near + k + 1, :]
                value = value + jnp.where(near == ids, weight, 0.0)
            high = value.astype(jnp.bfloat16)
            low = (value - high.astype(jnp.float32)).astype(jnp.bfloat16)
            put(j * sub, sub, high, low)

    def build_target(target):
        @pl.loop(0, n_img)
        def _(source):
            def put(at, count, high, low):
                wt[source, target, at : at + count] = high
                wt[source, target, rows + at : rows + at + count] = low

            build(target, source, put)

    def spread(p, b, first):
        piece = gath[p, b]
        twice = jnp.concatenate([piece, piece], axis=1)
        for s in range(n_img):
            got = jnp.dot(twice, wt[p, s], preferred_element_type=jnp.float32)
            if first:
                acc[s, b] = got
            else:
                acc[s, b] = acc[s, b] + got

    def spread_slot(p):
        for c in range(n_chunk):
            spread(p, my_r * n_chunk + c, False)
            sib_wait(p, c)
            spread(p, sib * n_chunk + c, False)

    def spread_own():
        @pl.loop(0, n_block)
        def _(b):
            spread(me, b, True)

    def spread_step(t):
        @pl.when(me >= t)
        def _():
            spread_slot(me - t)

        @pl.when(me + t < n_img)
        def _():
            spread_slot(me + t)

    if stored:
        build_target(me)

        def build_step(t):
            p = lax.rem(me + t, n_img)
            meta_wait(p)
            build_target(p)

        pending = [functools.partial(build_step, t) for t in range(1, n_img)]
        ready = [spread_own]
        for t in range(1, n_img):
            for c in range(n_chunk):
                event(t, c)
                if pending:
                    pending.pop(0)()
                else:
                    for job in ready:
                        job()
                    ready = []
            ready.append(functools.partial(spread_step, t))
        for job in pending + ready:
            job()
    else:
        for t in range(1, n_img):
            meta_wait(lax.rem(me + t, n_img))
            for c in range(n_chunk):
                event(t, c)
        for t in range(1, n_img):
            for c in range(n_chunk):

                @pl.when(me >= t)
                def _():
                    sib_wait(me - t, c)

                @pl.when(me + t < n_img)
                def _():
                    sib_wait(me + t, c)

        acc[...] = jnp.zeros_like(acc)

        @pl.loop(0, n_img)
        def _(source):
            @pl.loop(0, n_img)
            def _(target):
                def put(at, count, high, low):
                    wt[0, 0, at : at + count] = high
                    wt[0, 0, rows + at : rows + at + count] = low

                build(target, source, put)

                @pl.loop(0, n_block)
                def _(b):
                    piece = gath[source, b]
                    twice = jnp.concatenate([piece, piece], axis=1)
                    acc[target, b] = acc[target, b] + jnp.dot(
                        twice, wt[0, 0], preferred_element_type=jnp.float32
                    )

    def squares(s):
        total = jnp.zeros((1, rows), jnp.float32)
        for b in range(n_block):
            value = acc[s, b]
            total = total + jnp.sum(value * value, axis=0, keepdims=True)
        sqs[my_d, s] = total

    each(n_img, squares)

    def sq_copy(t):
        return pltpu.make_async_remote_copy(
            src_ref=sqs.at[my_d], dst_ref=sqs.at[my_d],
            send_sem=sq_send.at[t], recv_sem=sq_recv.at[my_d],
            device_id={"dsc": lax.rem(my_d + t, n_dsc)}, device_id_type=MESH,
        )

    for t in range(1, n_dsc):
        sq_copy(t).start()
    q_copy.wait()
    for t in range(1, n_dsc):
        p = lax.rem(my_d + t, n_dsc)
        pltpu.make_async_remote_copy(
            src_ref=sqs.at[p], dst_ref=sqs.at[p],
            send_sem=sq_send.at[t], recv_sem=sq_recv.at[p],
            device_id={"rep": sib}, device_id_type=MESH,
        ).wait_recv()

    def normalise(s):
        total = sqs[0, s]
        for d in range(1, n_dsc):
            total = total + sqs[d, s]
        scale = lax.rsqrt(total + epsilon)
        for b in range(n_block):
            augt[s, b * width : (b + 1) * width, :] = (acc[s, b] * scale).astype(jnp.bfloat16)

    each(n_img, normalise)

    def score(at):
        query = qv[at]
        listed = list_ref[at]
        chosen = [jnp.zeros((part_rows, BLK), jnp.float32) for _ in range(listed.shape[1])]
        for s in range(n_img):
            dense = jnp.dot(query, augt[s], preferred_element_type=jnp.float32)
            for u in range(rows // BLK):
                one = dense[:, u * BLK : (u + 1) * BLK]
                block = s * (rows // BLK) + u
                for column in range(len(chosen)):
                    chosen[column] = jnp.where(
                        listed[:, column : column + 1] == block, one, chosen[column]
                    )
        return jnp.concatenate(chosen, axis=1)

    def part_copy(t, part):
        p = lax.rem(my_d + t, n_dsc)
        return pltpu.make_async_remote_copy(
            src_ref=send_buf.at[p, part], dst_ref=recv_buf.at[my_d, part],
            send_sem=part_send.at[p, part], recv_sem=part_recv.at[my_d, part],
            device_id={"dsc": p}, device_id_type=MESH,
        )

    for t in range(1, n_dsc):
        p = lax.rem(my_d + t, n_dsc)
        for part in range(n_part):
            send_buf[p, part] = score(p * n_part + part).astype(jnp.bfloat16)
            part_copy(t, part).start()

    for part in range(n_part):
        score_out[part] = score(my_d * n_part + part)
    for b in range(n_block):
        aug_out[:, b * width : (b + 1) * width] = augt[me, b * width : (b + 1) * width, :].T

    for part in range(n_part):
        total = score_out[part]
        for t in range(1, n_dsc):
            p = lax.rem(my_d + t, n_dsc)
            pltpu.make_async_remote_copy(
                src_ref=send_buf.at[p, part], dst_ref=recv_buf.at[p, part],
                send_sem=part_send.at[p, part], recv_sem=part_recv.at[p, part],
                device_id={"dsc": p}, device_id_type=MESH,
            ).wait_recv()
            total = total + recv_buf[p, part].astype(jnp.float32)
        score_out[part] = total

    for t in range(1, n_img):
        meta_copy(t).wait_send()
    if not stored or n_img < 2:
        pass
    for t in range(1, n_dsc):
        sq_copy(t).wait_send()
        for part in range(n_part):
            part_copy(t, part).wait_send()
    for c in range(n_chunk):

        @pl.when(has_right)
        def _():
            z_copy(me, c, 1).wait_send()

        @pl.when(has_left)
        def _():
            z_copy(me, c, -1).wait_send()

        for t in range(1, n_img):

            @pl.when(me >= t)
            def _():
                @pl.when(has_right)
                def _():
                    z_copy(me - t, c, 1).wait_send()

                sib_copy(me - t, c).wait_send()

            @pl.when(me + t < n_img)
            def _():
                @pl.when(has_left)
                def _():
                    z_copy(me + t, c, -1).wait_send()

                sib_copy(me + t, c).wait_send()


def per_device(images, neighbours, similarity, queries, shortlist):
    n_img, n_dsc = lax.axis_size("img"), lax.axis_size("dsc")
    rows, columns = images.shape
    n_near = neighbours.shape[1]
    own = queries.shape[0] // (n_img * n_dsc)
    part_rows = min(own, 128)
    n_part = own // part_rows
    n_chunk = 2 if columns // 4 >= 128 else 1
    width = columns // (2 * n_chunk)
    n_block = 2 * n_chunk
    stored = n_img <= 4
    pad = -2 * n_near % 8
    meta = jnp.concatenate(
        [
            (similarity**3).T,
            neighbours.T.astype(jnp.float32),
            jnp.zeros((pad, rows), jnp.float32),
        ],
        axis=0,
    )
    listed = lax.dynamic_index_in_dim(
        shortlist.reshape(n_img, n_dsc * n_part, part_rows, shortlist.shape[1]),
        lax.axis_index("img"), 0, keepdims=False,
    )
    answers = shortlist.shape[1] * BLK
    n_wt = n_img if stored else 1
    dma = pltpu.SemaphoreType.DMA
    vmem = pl.BlockSpec(memory_space=pltpu.VMEM)
    augmented, scores = pl.pallas_call(
        functools.partial(kernel, n_img, n_dsc, n_near, n_chunk, n_part, stored),
        out_shape=(
            jax.ShapeDtypeStruct((rows, columns), jnp.bfloat16),
            jax.ShapeDtypeStruct((n_part, part_rows, answers), jnp.float32),
        ),
        in_specs=[vmem, vmem, vmem, pl.BlockSpec(memory_space=pl.ANY)],
        out_specs=(vmem, vmem),
        scratch_shapes=[
            pltpu.VMEM((n_img, n_block, width, rows), jnp.bfloat16),
            pltpu.VMEM((n_img,) + meta.shape, jnp.float32),
            pltpu.VMEM((n_wt, n_wt, 2 * rows, rows), jnp.bfloat16),
            pltpu.VMEM((n_img, n_block, width, rows), jnp.float32),
            pltpu.VMEM((n_img, columns, rows), jnp.bfloat16),
            pltpu.VMEM((n_dsc, n_img, 1, rows), jnp.float32),
            pltpu.VMEM((n_dsc * n_part, part_rows, columns), jnp.bfloat16),
            pltpu.VMEM((n_dsc, n_part, part_rows, answers), jnp.bfloat16),
            pltpu.VMEM((n_dsc, n_part, part_rows, answers), jnp.bfloat16),
            dma,
            dma((n_img,)),
            dma((n_img,)),
            dma((n_img, n_chunk)),
            dma((n_img, n_chunk)),
            dma((n_img, n_chunk)),
            dma((n_img, n_chunk)),
            dma((n_img, n_chunk)),
            dma((n_dsc,)),
            dma((n_dsc,)),
            dma((n_dsc, n_part)),
            dma((n_dsc, n_part)),
        ],
        compiler_params=pltpu.CompilerParams(
            collective_id=0, has_side_effects=True, vmem_limit_bytes=40 * 1024 * 1024
        ),
    )(
        images, meta, listed,
        queries.reshape(n_img, n_dsc * n_part, part_rows, columns),
    )
    return augmented, scores.reshape(1, own, answers)


def solution(mesh):
    placed = (
        P(("groups", "img"), "dsc"),
        P(("groups", "img"), None),
        P(("groups", "img"), None),
        P(("groups", "rep"), "dsc"),
        P(("groups", "rep"), None),
    )
    return jax.shard_map(
        per_device,
        mesh=mesh,
        in_specs=placed,
        out_specs=(P(("groups", "img"), "dsc"), P("rep", ("groups", "img", "dsc"), None)),
        check_vma=False,
    )
```

time: 553 us -> 45.5 us (0.08)
  waiting for transfers between devices: 312 us -> 0 us
  local copies, waits for them, and re-layouts: 108 us -> 6.55 us
  matrix products: 49.6 us -> 0 us
  other arithmetic: 44.3 us -> 0.09 us
  Pallas kernels: 0 us -> 38 us
  blocking collectives: 16.7 us -> 0 us
  between operations: 14.2 us -> 0.73 us
  starting transfers between devices: 6.16 us -> 0 us
    all_to_all x1 -> x0, waiting for transfers between devices: 225 us -> none  [fetch_rows(): lax.all_to_all(picked, 'img', split_axis=0, concat_axis=0, tiled=True)]
    reduce_scatter x1 -> x0, waiting for transfers between devices: 87.2 us -> none  [per_device(): lax.psum_scatter(lax.map(score_block, (query_blocks, list_blocks)).reshap...]
    gather x2 -> x0, local copies, waits for them, and re-layouts: 74.2 us -> none  [the longest x1 51.6 us: fetch_rows(): gathered = fetched[owner, slot]]
    dot_general x16 -> x0, matrix products: 49.6 us -> none  [the longest x8 36 us: score_block(): jnp.einsum('qsp,qpb->qsb', select, dense, precision=lax.Precision.HIGHEST)]
    pallas_call x0 -> x1, Pallas kernels: none -> 38 us  [per_device(): pl.pallas_call(functools.partial(kernel, n_img, n_dsc, n_near, n_chunk, n...]
    slice x1 -> x0, other arithmetic: 20.8 us -> none  [blend_rows(): picked[:, column].astype(jnp.float32)]
    all_to_all x1 -> x0, blocking collectives: 11.7 us -> none  [fetch_rows(): lax.all_to_all(request, 'img', split_axis=0, concat_axis=0, tiled=True)]
    select_n x4 -> x0, other arithmetic: 10.2 us -> none  [the longest x2 10.1 us: fetch_rows(): jnp.take(images, lax.all_to_all(request, 'img', split_axis=0, concat_axis...]
  transfers between devices with their start and end apart: 2 -> 0, of which waited for: 2 -> 0; matrix products, arithmetic and copies ran while one was open for 0% -> 0% of each run, Pallas kernels for 0% -> 0%
where the time goes in v1:
time: 45.5 us; the launch traced here: 45.4 us
  Pallas kernels  38 us (84%)
  local copies, waits for them, and re-layouts  6.55 us (14%)
  between operations  0.73 us (2%)
    pallas_call x1, Pallas kernels, per_device(): pl.pallas_call(functools.partial(kernel, n_img, n_dsc, n_near, n_chunk, n...  38 us
    unnamed x10, local copies, waits for them, and re-layouts  4.98 us
    reshape x1, local copies, waits for them, and re-layouts, per_device(): shortlist.reshape(n_img, n_dsc * n_part, part_rows, shortlist.shape[1])  1.45 us

profile of v1, /device:TPU:0, one launch (start us, length us, event | category | flops | bytes accessed | tf_op | source)
XLA Modules:
  0.0 45.4 jit_solution(15737757127837194762)
XLA Ops:
  0.6 0.0 copy-start.2
  0.6 0.0 copy-start.3
  0.7 0.0 copy-start.1
  0.7 1.4 %copy.8 = s32[4096,2]{1,0:T(8,128)S(1)} copy(s32[4096,2]{0,1:T(2,128)} %param.9) | data formatting | bytes 65536 | tf_op jit(solution)/shard_map/reshape | solution.py:396
  2.2 0.0 copy-done.2
  2.2 0.0 copy-done.3
  2.2 0.1 pad.2.clone
  2.3 0.1 maximum_maximum_fusion.meta_ref
  2.4 0.0 copy-done.1
  2.4 0.0 copy-start
  2.4 3.4 %copy-done = bf16[4096,1024]{1,0:T(8,128)(2,1)S(1)} copy-done((bf16[4096,1024]{1,0:T(8,128)(2,1)S(1)}, bf16[4096,1024]{1,0:T(8,128)(2,1)}, u32[]{:S(2)}) %copy-start) | copy-done | bytes 8388632
  5.8 38.0 %shard_map.68 = (bf16[256,1024]{1,0:T(8,128)(2,1)S(1)}, f32[4,128,256]{2,1,0:T(8,128)S(1)}) custom-call(bf16[256,1024]{1,0:T(8,128)(2,1)S(1)} %copy-done.1, f32[24,256]{1,0:T(8,128)S(1)} %maximum_maximum_fusion.meta_ref, s32[8,128,2]{2,1,0:T(8,128)S(1)} %dynamic-slice_bitcast_fusion.list_ref, bf16[4,8,128,1024]{3,2,1,0:T(8,128)(2,1)S(1)} %bitcast.9), custom_call_target="tpu_custom_call" | custom-call | tf_op jit(solution)/shard_map/pallas_call | solution.py:403
  43.8 0.8 %copy.11 = bf16[256,1024]{1,0:T(8,128)(2,1)} copy(bf16[256,1024]{1,0:T(8,128)(2,1)S(1)} %get-tuple-element.8) | data formatting | bytes 1048576
  44.6 0.8 %copy.12 = f32[1,512,256]{2,1,0:T(8,128)} copy(f32[1,512,256]{2,1,0:T(8,128)S(1)} %bitcast.10) | data formatting | bytes 1048576
  (4 shorter events, 0.1 us)
Async XLA Ops:
  0.6 1.5 %copy-start.2 = (s32[256,10]{0,1:T(8,128)S(1)}, s32[256,10]{0,1:T(8,128)}, u32[]{:S(2)}) copy-start(s32[256,10]{0,1:T(8,128)} %param.6) | copy-start | bytes 30724
  0.6 1.6 %copy-start.3 = (f32[256,10]{0,1:T(8,128)S(1)}, f32[256,10]{0,1:T(8,128)}, u32[]{:S(2)}) copy-start(f32[256,10]{0,1:T(8,128)} %param.7) | copy-start | bytes 30724
  0.7 1.7 %copy-start.1 = (bf16[256,1024]{1,0:T(8,128)(2,1)S(1)}, bf16[256,1024]{1,0:T(8,128)(2,1)}, u32[]{:S(2)}) copy-start(bf16[256,1024]{1,0:T(8,128)(2,1)} %img_ref.1) | copy-start | bytes 1572868
  2.4 3.4 %copy-start = (bf16[4096,1024]{1,0:T(8,128)(2,1)S(1)}, bf16[4096,1024]{1,0:T(8,128)(2,1)}, u32[]{:S(2)}) copy-start(bf16[4096,1024]{1,0:T(8,128)(2,1)} %param.8) | copy-start | bytes 25165828

commit v2 on v1

--- a/solution.py
+++ b/solution.py
@@ -29,7 +29,7 @@
     n_img, n_dsc, n_near, n_chunk, n_part, stored,
     img_ref, meta_ref, list_ref, q_hbm,
     aug_out, score_out,
-    gath, metas, wt, acc, augt, sqs, qv, send_buf, recv_buf,
+    listed, gath, metas, wt, acc, augt, sqs, qv, send_buf, recv_buf,
     q_sem, meta_send, meta_recv, z_right, z_left, z_recv, sib_send, sib_recv,
     sq_send, sq_recv, part_send, part_recv,
 ):
@@ -174,26 +174,33 @@
             else:
                 acc[s, b] = acc[s, b] + got
 
-    def spread_slot(p):
-        for c in range(n_chunk):
-            spread(p, my_r * n_chunk + c, False)
-            sib_wait(p, c)
-            spread(p, sib * n_chunk + c, False)
+    def spread_slot(p, c):
+        spread(p, my_r * n_chunk + c, False)
+        sib_wait(p, c)
+        spread(p, sib * n_chunk + c, False)
 
     def spread_own():
         @pl.loop(0, n_block)
         def _(b):
             spread(me, b, True)
 
-    def spread_step(t):
+    def spread_step(t, c):
         @pl.when(me >= t)
         def _():
-            spread_slot(me - t)
+            spread_slot(me - t, c)
 
         @pl.when(me + t < n_img)
         def _():
-            spread_slot(me + t)
-
+            spread_slot(me + t, c)
+
+    def spread_list():
+        for column in range(list_ref.shape[0]):
+            for j in range(list_ref.shape[1] // 128):
+                span = slice(j * 128, (j + 1) * 128)
+                line = list_ref[column : column + 1, span].astype(jnp.float32)
+                listed[column, span, :] = jnp.broadcast_to(line, (128, 128)).T
+
+    spread_list()
     if stored:
         build_target(me)
 
@@ -213,7 +220,7 @@
                     for job in ready:
                         job()
                     ready = []
-            ready.append(functools.partial(spread_step, t))
+                ready.append(functools.partial(spread_step, t, c))
         for job in pending + ready:
             job()
     else:
@@ -291,17 +298,16 @@
 
     def score(at):
         query = qv[at]
-        listed = list_ref[at]
-        chosen = [jnp.zeros((part_rows, BLK), jnp.float32) for _ in range(listed.shape[1])]
+        span = pl.ds(pl.multiple_of(at * part_rows, part_rows), part_rows)
+        asked = [listed[column, span, :] for column in range(list_ref.shape[0])]
+        chosen = [jnp.zeros((part_rows, BLK), jnp.float32) for _ in asked]
         for s in range(n_img):
             dense = jnp.dot(query, augt[s], preferred_element_type=jnp.float32)
             for u in range(rows // BLK):
                 one = dense[:, u * BLK : (u + 1) * BLK]
                 block = s * (rows // BLK) + u
                 for column in range(len(chosen)):
-                    chosen[column] = jnp.where(
-                        listed[:, column : column + 1] == block, one, chosen[column]
-                    )
+                    chosen[column] = jnp.where(asked[column] == block, one, chosen[column])
         return jnp.concatenate(chosen, axis=1)
 
     def part_copy(t, part):
@@ -337,8 +343,6 @@
 
     for t in range(1, n_img):
         meta_copy(t).wait_send()
-    if not stored or n_img < 2:
-        pass
     for t in range(1, n_dsc):
         sq_copy(t).wait_send()
         for part in range(n_part):
@@ -392,9 +396,8 @@
         ],
         axis=0,
     )
-    listed = lax.dynamic_index_in_dim(
-        shortlist.reshape(n_img, n_dsc * n_part, part_rows, shortlist.shape[1]),
-        lax.axis_index("img"), 0, keepdims=False,
+    listed = lax.dynamic_slice_in_dim(
+        shortlist.T, lax.axis_index("img") * n_dsc * own, n_dsc * own, axis=1
     )
     answers = shortlist.shape[1] * BLK
     n_wt = n_img if stored else 1
@@ -409,6 +412,7 @@
         in_specs=[vmem, vmem, vmem, pl.BlockSpec(memory_space=pl.ANY)],
         out_specs=(vmem, vmem),
         scratch_shapes=[
+            pltpu.VMEM(listed.shape + (BLK,), jnp.float32),
             pltpu.VMEM((n_img, n_block, width, rows), jnp.bfloat16),
             pltpu.VMEM((n_img,) + meta.shape, jnp.float32),
             pltpu.VMEM((n_wt, n_wt, 2 * rows, rows), jnp.bfloat16),
@@ -432,7 +436,7 @@
             dma((n_dsc, n_part)),
         ],
         compiler_params=pltpu.CompilerParams(
-            collective_id=0, has_side_effects=True, vmem_limit_bytes=40 * 1024 * 1024
+            collective_id=0, has_side_effects=True, vmem_limit_bytes=52 * 1024 * 1024
         ),
     )(
         images, meta, listed,

time: 45.5 us -> 44.2 us (0.971)
  local copies, waits for them, and re-layouts: 6.55 us -> 3.37 us
  other arithmetic: 0.09 us -> 1.51 us
    unnamed x10 -> x6, local copies, waits for them, and re-layouts: 4.98 us -> 3.29 us
    reshape x1 -> x0, local copies, waits for them, and re-layouts: 1.45 us -> none  [per_device(): shortlist.reshape(n_img, n_dsc * n_part, part_rows, shortlist.shape[1])]
    convert_element_type x1, other arithmetic: 0.01 us -> 0.72 us  [per_device(): neighbours.T.astype(jnp.float32)]
    transpose x1, other arithmetic: 0.01 us -> 0.72 us  [per_device(): meta = jnp.concatenate([(similarity ** 3).T, neighbours.T.astype(jnp.floa...]
where the time goes in v2:
time: 44.2 us; the launch traced here: 43.9 us
  Pallas kernels  38.3 us (87%)
  local copies, waits for them, and re-layouts  3.37 us (8%)
  other arithmetic  1.51 us (3%)
  between operations  0.66 us (1%)
    pallas_call x1, Pallas kernels, per_device(): pl.pallas_call(functools.partial(kernel, n_img, n_dsc, n_near, n_chunk, n...  38.3 us
    unnamed x6, local copies, waits for them, and re-layouts  3.29 us

profile of v2, /device:TPU:0, one launch (start us, length us, event | category | flops | bytes accessed | tf_op | source)
XLA Modules:
  0.0 43.9 jit_solution(9441676903660239604)
XLA Ops:
  0.6 0.0 copy-start
  0.7 0.1 pad.2.clone
  0.7 0.7 %copy-done = s32[4096,2]{0,1:T(2,128)S(1)} copy-done((s32[4096,2]{0,1:T(2,128)S(1)}, s32[4096,2]{0,1:T(2,128)}, u32[]{:S(2)}) %copy-start) | copy-done | bytes 32792
  1.4 0.7 %convert_bitcast_fusion = f32[10,256]{1,0:T(8,128)S(1)} fusion(s32[256,10]{0,1:T(8,128)} %param.6), kind=kLoop, calls=%fused_computation.3 | loop fusion | flops 2560 | bytes 20480 | tf_op jit(solution)/shard_map/convert_element_type | solution.py:394
  2.1 0.7 %fusion = f32[10,256]{1,0:T(8,128)S(1)} fusion(f32[256,10]{0,1:T(8,128)} %param.7), kind=kLoop, calls=%fused_computation.2 | loop fusion | flops 5120 | bytes 20480 | tf_op jit(solution)/shard_map/transpose | solution.py:393
  2.8 0.1 maximum_maximum_fusion.meta_ref
  2.9 0.0 copy-start.1
  2.9 1.0 %copy-done.1 = bf16[256,1024]{1,0:T(8,128)(2,1)S(1)} copy-done((bf16[256,1024]{1,0:T(8,128)(2,1)S(1)}, bf16[256,1024]{1,0:T(8,128)(2,1)}, u32[]{:S(2)}) %copy-start.1) | copy-done | bytes 524312
  4.0 38.3 %shard_map.68 = (bf16[256,1024]{1,0:T(8,128)(2,1)S(1)}, f32[4,128,256]{2,1,0:T(8,128)S(1)}) custom-call(bf16[256,1024]{1,0:T(8,128)(2,1)S(1)} %copy-done.1, f32[24,256]{1,0:T(8,128)S(1)} %maximum_maximum_fusion.meta_ref, s32[2,1024]{1,0:T(2,128)S(1)} %dynamic-slice_bitcast_fusion.list_ref, bf16[4,8,128,1024]{3,2,1,0:T(8,128)(2,1)} %bitcast.9), custom_call_target="tpu_custom_call" | custom-call | tf_op jit(solution)/shard_map/pallas_call | solution.py:406
  42.3 0.8 %copy.9 = bf16[256,1024]{1,0:T(8,128)(2,1)} copy(bf16[256,1024]{1,0:T(8,128)(2,1)S(1)} %get-tuple-element.8) | data formatting | bytes 1048576
  43.1 0.8 %copy.10 = f32[1,512,256]{2,1,0:T(8,128)} copy(f32[1,512,256]{2,1,0:T(8,128)S(1)} %bitcast.8) | data formatting | bytes 1048576
  (2 shorter events, 0.0 us)
Async XLA Ops:
  0.6 0.8 %copy-start = (s32[4096,2]{0,1:T(2,128)S(1)}, s32[4096,2]{0,1:T(2,128)}, u32[]{:S(2)}) copy-start(s32[4096,2]{0,1:T(2,128)} %param.9) | copy-start | bytes 98308
  2.9 1.0 %copy-start.1 = (bf16[256,1024]{1,0:T(8,128)(2,1)S(1)}, bf16[256,1024]{1,0:T(8,128)(2,1)}, u32[]{:S(2)}) copy-start(bf16[256,1024]{1,0:T(8,128)(2,1)} %img_ref.1) | copy-start | bytes 1572868

commit v3 on v2

--- a/solution.py
+++ b/solution.py
@@ -214,13 +214,13 @@
         for t in range(1, n_img):
             for c in range(n_chunk):
                 event(t, c)
+                ready.append(functools.partial(spread_step, t, c))
                 if pending:
                     pending.pop(0)()
                 else:
                     for job in ready:
                         job()
                     ready = []
-                ready.append(functools.partial(spread_step, t, c))
         for job in pending + ready:
             job()
     else:

time: 44.2 us -> 45.1 us (1.020)
  Pallas kernels: 38.3 us -> 39.2 us
    pallas_call x1, Pallas kernels: 38.3 us -> 39.2 us  [per_device(): pl.pallas_call(functools.partial(kernel, n_img, n_dsc, n_near, n_chunk, n...]
where the time goes in v3:
time: 45.1 us; the launch traced here: 44.7 us
  Pallas kernels  39.2 us (87%)
  local copies, waits for them, and re-layouts  3.37 us (7%)
  other arithmetic  1.51 us (3%)
  between operations  0.66 us (1%)
    pallas_call x1, Pallas kernels, per_device(): pl.pallas_call(functools.partial(kernel, n_img, n_dsc, n_near, n_chunk, n...  39.2 us
    unnamed x6, local copies, waits for them, and re-layouts  3.29 us

profile of v3, /device:TPU:0, one launch (start us, length us, event | category | flops | bytes accessed | tf_op | source)
XLA Modules:
  0.0 44.7 jit_solution(768303670866820230)
XLA Ops:
  0.6 0.0 copy-start
  0.7 0.1 pad.2.clone
  0.7 0.7 %copy-done = s32[4096,2]{0,1:T(2,128)S(1)} copy-done((s32[4096,2]{0,1:T(2,128)S(1)}, s32[4096,2]{0,1:T(2,128)}, u32[]{:S(2)}) %copy-start) | copy-done | bytes 32792
  1.4 0.7 %convert_bitcast_fusion = f32[10,256]{1,0:T(8,128)S(1)} fusion(s32[256,10]{0,1:T(8,128)} %param.6), kind=kLoop, calls=%fused_computation.3 | loop fusion | flops 2560 | bytes 20480 | tf_op jit(solution)/shard_map/convert_element_type | solution.py:394
  2.1 0.7 %fusion = f32[10,256]{1,0:T(8,128)S(1)} fusion(f32[256,10]{0,1:T(8,128)} %param.7), kind=kLoop, calls=%fused_computation.2 | loop fusion | flops 5120 | bytes 20480 | tf_op jit(solution)/shard_map/transpose | solution.py:393
  2.8 0.1 maximum_maximum_fusion.meta_ref
  2.9 0.0 copy-start.1
  2.9 1.0 %copy-done.1 = bf16[256,1024]{1,0:T(8,128)(2,1)S(1)} copy-done((bf16[256,1024]{1,0:T(8,128)(2,1)S(1)}, bf16[256,1024]{1,0:T(8,128)(2,1)}, u32[]{:S(2)}) %copy-start.1) | copy-done | bytes 524312
  4.0 39.2 %shard_map.68 = (bf16[256,1024]{1,0:T(8,128)(2,1)S(1)}, f32[4,128,256]{2,1,0:T(8,128)S(1)}) custom-call(bf16[256,1024]{1,0:T(8,128)(2,1)S(1)} %copy-done.1, f32[24,256]{1,0:T(8,128)S(1)} %maximum_maximum_fusion.meta_ref, s32[2,1024]{1,0:T(2,128)S(1)} %dynamic-slice_bitcast_fusion.list_ref, bf16[4,8,128,1024]{3,2,1,0:T(8,128)(2,1)} %bitcast.9), custom_call_target="tpu_custom_call" | custom-call | tf_op jit(solution)/shard_map/pallas_call | solution.py:406
  43.1 0.8 %copy.9 = bf16[256,1024]{1,0:T(8,128)(2,1)} copy(bf16[256,1024]{1,0:T(8,128)(2,1)S(1)} %get-tuple-element.8) | data formatting | bytes 1048576
  43.9 0.8 %copy.10 = f32[1,512,256]{2,1,0:T(8,128)} copy(f32[1,512,256]{2,1,0:T(8,128)S(1)} %bitcast.8) | data formatting | bytes 1048576
  (2 shorter events, 0.0 us)
Async XLA Ops:
  0.6 0.8 %copy-start = (s32[4096,2]{0,1:T(2,128)S(1)}, s32[4096,2]{0,1:T(2,128)}, u32[]{:S(2)}) copy-start(s32[4096,2]{0,1:T(2,128)} %param.9) | copy-start | bytes 98308
  2.9 1.0 %copy-start.1 = (bf16[256,1024]{1,0:T(8,128)(2,1)S(1)}, bf16[256,1024]{1,0:T(8,128)(2,1)}, u32[]{:S(2)}) copy-start(bf16[256,1024]{1,0:T(8,128)(2,1)} %img_ref.1) | copy-start | bytes 1572868
